TPU v7x, 32 devices: a whole 2x2x4 slice. The times are simulated.
32 devices in a mesh: variant: 2 (over x), elem: 4 (over y, core), sub: 4 (over z).
Axes of the slice: x: 2, y: 2, z: 4, core: 2. Of those that a mesh axis runs over, the one named last changes fastest.
Arguments:
- right_side: float32 [8192, 512], P(('variant', 'elem', 'sub')), parts along dimension 0, may hold values from -16 to 16, as said below
- smoother_scale: float32 [8192, 512], P(('variant', 'elem', 'sub')), parts along dimension 0, may hold values from 0.5 to 1.5
- helmholtz: float32 [8192, 512], P(('variant', 'elem', 'sub')), parts along dimension 0, may hold values from 0.5 to 2
- geometry: float32 [3, 8192, 512], P(None, ('variant', 'elem', 'sub')), parts along dimension 1, may hold values from 0.001 to 0.01
- coarse_inverse: float32 [8, 1024, 1024], P(('variant', 'elem'), 'sub'), parts along dimension 0, may hold values from -1.25 to 6.25, as said below
- vertex_ids: int32 [8, 4096], P(None, ('elem', 'sub')), may hold values from 0 to 1023
- face_slot: int32 [16, 4, 192], P(('elem', 'sub')), may hold values from 0 to 1535, as said below
- face_partner: int32 [16, 4, 192], P(('elem', 'sub')), may hold values from 0 to 191, as said below
Outputs:
- solution: float32 [8192, 512], P(('variant', 'elem', 'sub')), parts along dimension 0
- residual: float32 [8192, 512], P(('variant', 'elem', 'sub')), parts along dimension 0
- direction: float32 [8192, 512], P(('variant', 'elem', 'sub')), parts along dimension 0
There are 2 independent parts, one for each index of `variant`. A program takes and returns all parts, laid end to end along the dimension named above; an argument that names none is the same for every part. Nothing has to cross between parts.
Inputs may be any that keep to these rules, and one draw needn't show every extreme that they name: `right_side`: Right-hand side values; their size differs from device to device. `coarse_inverse`: each matrix is symmetric. `vertex_ids`: vertex v of a coarse group belongs to index v // 256 of sub. Each device's corners may name any vertex of its group. `face_slot`: the 768 entries of one device are all different. For every device and section the row is a permutation of 0 to 191, and the pairing is mutual: face_partner[d XOR 2^b, b, face_partner[d, b, k]] = k.
All inputs are finite; a program needn't handle non-finite values.
Results may differ from a plain program's by a relative error of at most 0.0003.
Values sent between devices are 32-bit elements; how exact they have to be, the bound alone decides.
A program may use at most 128 MiB of HBM per device.

v0:
```python
import jax
import jax.numpy as jnp
import numpy as np
from jax import lax
from jax.sharding import PartitionSpec as P

NP = 8
ITERS = 2


PENALTY = 1.0
SMOOTH = 0.125


def from_partner(x, axis, distance):
    return lax.ppermute(x, axis, [(i, i ^ 1 << distance) for i in range(lax.axis_size(axis))])


def derivative_table(points):
    nodes = -np.cos(np.pi * np.arange(points) / (points - 1))
    end_weights = np.ones(points)
    end_weights[0] = 2.0
    end_weights[-1] = 2.0
    table = np.zeros((points, points))
    for row_index in range(points):
        for column in range(points):
            if row_index != column:
                table[row_index, column] = (
                    end_weights[row_index]
                    / end_weights[column]
                    * (-1.0) ** (row_index + column)
                    / (nodes[row_index] - nodes[column])
                )
        table[row_index, row_index] = -np.sum(table[row_index])
    return (nodes, table)


def spectral_tables(points):
    nodes, deriv = derivative_table(points)
    unit = np.eye(points)
    slow_op = np.kron(deriv, np.kron(unit, unit))
    middle_op = np.kron(unit, np.kron(deriv, unit))
    fast_op = np.kron(unit, np.kron(unit, deriv))
    operators = np.stack([slow_op, middle_op, fast_op])
    hats = np.stack([(1.0 - nodes) / 2.0, (1.0 + nodes) / 2.0])
    turned = hats.T
    raw_hats = (
        turned[:, None, None, :, None, None]
        * turned[None, :, None, None, :, None]
        * turned[None, None, :, None, None, :]
    )
    raw_hats = raw_hats.reshape(points**3, 8)
    corner = raw_hats / raw_hats.sum(axis=0, keepdims=True)
    grid = np.arange(points**3).reshape(points, points, points)
    sides = np.stack(
        [
            grid[0].ravel(),
            grid[-1].ravel(),
            grid[:, 0].ravel(),
            grid[:, -1].ravel(),
            grid[:, :, 0].ravel(),
            grid[:, :, -1].ravel(),
        ]
    )
    return (
        jnp.asarray(operators, jnp.float32),
        jnp.asarray(corner, jnp.float32),
        jnp.asarray(raw_hats, jnp.float32),
        sides,
    )


def stiffness(field, geometry, helmholtz, operators):
    total = helmholtz * field
    for direction_index in range(3):
        slope = jnp.dot(field, operators[direction_index].T, precision=lax.Precision.HIGHEST)
        total = total + jnp.dot(
            geometry[direction_index] * slope,
            operators[direction_index],
            precision=lax.Precision.HIGHEST,
        )
    return total


def face_values(field, slots, sides):
    stacked = jnp.concatenate([field[:, sides[side_number]] for side_number in range(6)], axis=0)
    return jnp.take(stacked, slots, axis=0)


def spread_faces(values, slots, sides, count):
    square = sides.shape[1]
    flat = (
        jnp.zeros((6 * count, square), values.dtype)
        .at[slots.reshape(-1)]
        .add(values.reshape(-1, square))
    )
    result = jnp.zeros((count, square * NP), values.dtype)
    for side_number in range(6):
        result = result.at[:, sides[side_number]].add(
            flat[side_number * count : (side_number + 1) * count]
        )
    return result


def neighbour_sum(field, slots, partners, sides):
    faces = face_values(field, slots, sides)
    sections, width, square = faces.shape
    packed = faces.reshape(sections, width * square // 128, 128)
    received = jnp.stack(
        [from_partner(packed[section], ("elem", "sub"), section) for section in range(sections)]
    )
    received = received.reshape(sections, width, square)
    aligned = jnp.take_along_axis(received, partners[:, :, None], axis=1)
    return spread_faces(aligned, slots, sides, field.shape[0])


def coarse_term(resid, vertex_ids, coarse_rows, corner, prolong):
    corners = jnp.dot(resid, corner, precision=lax.Precision.HIGHEST)
    partial_rhs = jax.ops.segment_sum(
        corners.T.reshape(-1), vertex_ids.reshape(-1), num_segments=coarse_rows.shape[1]
    )
    whole_rhs = lax.psum(partial_rhs, "sub")
    solved = jnp.dot(coarse_rows, whole_rhs, precision=lax.Precision.HIGHEST)
    everywhere = lax.all_gather(solved, "sub", axis=0, tiled=True)
    picked = jnp.take(everywhere, vertex_ids, axis=0)
    return jnp.dot(picked.T, prolong.T, precision=lax.Precision.HIGHEST)


def inner_total(product):
    return lax.psum(jnp.sum(product), ("elem", "sub"))


def on_device(
    right_side,
    smoother_scale,
    helmholtz,
    geometry,
    coarse_inverse,
    vertex_ids,
    face_slot,
    face_partner,
):
    operators, corner, prolong, sides = spectral_tables(NP)
    slots = face_slot[0]
    partners = face_partner[0]
    coarse_rows = coarse_inverse[0]
    count = right_side.shape[0]
    degree = spread_faces(
        jnp.ones(slots.shape + (sides.shape[1],), right_side.dtype), slots, sides, count
    )

    def precondition(resid):
        scaled = smoother_scale * resid
        smooth = scaled - SMOOTH * (degree * scaled - neighbour_sum(scaled, slots, partners, sides))
        return smoother_scale * smooth + coarse_term(
            resid, vertex_ids, coarse_rows, corner, prolong
        )

    solution = jnp.zeros_like(right_side)
    residual = right_side
    precond = precondition(residual)
    direction = precond
    rz_now = inner_total(residual * precond)
    for sweep in range(ITERS):
        coupled = degree * direction - neighbour_sum(direction, slots, partners, sides)
        image = stiffness(direction, geometry, helmholtz, operators) + PENALTY * coupled
        alpha = rz_now / inner_total(direction * image)
        solution = solution + alpha * direction
        residual = residual - alpha * image
        precond = precondition(residual)
        rz_next = inner_total(residual * precond)
        direction = precond + rz_next / rz_now * direction
        rz_now = rz_next
    return (solution, residual, direction)


def solution(mesh):
    in_specs = (
        P(("variant", "elem", "sub"), None),
        P(("variant", "elem", "sub"), None),
        P(("variant", "elem", "sub"), None),
        P(None, ("variant", "elem", "sub"), None),
        P(("variant", "elem"), "sub", None),
        P(None, ("elem", "sub")),
        P(("elem", "sub"), None, None),
        P(("elem", "sub"), None, None),
    )
    out_specs = (
        P(("variant", "elem", "sub"), None),
        P(("variant", "elem", "sub"), None),
        P(("variant", "elem", "sub"), None),
    )
    return jax.shard_map(
        on_device, mesh=mesh, in_specs=in_specs, out_specs=out_specs, check_vma=False
    )
```

profile of v0, /device:TPU:0, one launch (start us, length us, event | category | flops | bytes accessed | tf_op | source)
XLA Modules:
  0.0 570.3 jit_solution(13213374049434159842)
XLA Ops:
  10.8 3.0 collective-permute-start.3
  15.2 2.6 collective-permute-start.1
  22.5 5.7 %scatter_custom_fusion = f32[1536,64]{1,0:T(8,128)S(1)} fusion(s32[768]{0:T(1024)S(1)} %fusion.37, f32[]{:T(128)} %constant.22.clone.1, f32[]{:T(128)} %constant.43.clone.1), kind=kCustom, calls=%fused_computation.139 | custom fusion | flops 49152 | bytes 393224 | tf_op jit(solution)/shard_map/scatter-add | solution.py:95
  29.6 14.7 %scatter_custom_fusion.14 = f32[1024]{0:T(1024)S(1)} fusion(s32[2048]{0:T(1024)S(1)} %bitcast.272, f32[2048]{0:T(1024)S(1)} %bitcast.276, f32[]{:T(128)} %constant.22.clone.1), kind=kCustom, calls=%fused_computation.258 | custom fusion | flops 2048 | bytes 4100 | tf_op jit(solution)/shard_map/scatter-add | solution.py:119
  44.3 8.8 %psum.56 = f32[1024]{0:T(1024)S(1)} all-reduce(f32[1024]{0:T(1024)S(1)} %scatter_custom_fusion.14), channel_id=1, replica_groups=mesh['variant'=2,'elem'=4,'sub'=4] {'sub'}, use_global_device_ids=true, to_apply=%region_15.18 | all-reduce | flops 1024 | bytes 8192 | tf_op jit(solution)/shard_map/psum | solution.py:122
  62.5 9.3 %all-gather = f32[4,1,256]{2,1,0:T(1,128)S(1)} all-gather(f32[1,1,256]{2,1,0:T(1,128)S(1)} %convolution_bitcast_fusion.5), channel_id=1, replica_groups=mesh['variant'=2,'elem'=4,'sub'=4] {'sub'}, dimensions={0}, use_global_device_ids=true | all-gather | bytes 5120 | tf_op jit(solution)/shard_map/all_gather | solution.py:124
  71.9 8.6 %gather_fusion.32 = f32[2048]{0:T(1024)S(1)} fusion(f32[1024]{0:T(1024)S(1)} %bitcast.250, s32[2048]{0:T(1024)S(1)} %broadcast_clamp_fusion), kind=kCustom, calls=%fused_computation.2.clone | custom fusion | bytes 24576 | tf_op jit(solution)/shard_map/jit(_take)/gather | solution.py:125
  84.1 5.2 gather_fusion.31
  89.5 7.1 %scatter_custom_fusion.7 = f32[1536,64]{1,0:T(8,128)} fusion(s32[768]{0:T(1024)} %copy-done.80, f32[768,64]{1,0:T(8,128)S(1)} %bitcast.263, f32[]{:T(128)} %constant.22.clone.1), kind=kCustom, calls=%fused_computation.137 | custom fusion | flops 49152 | bytes 393728 | tf_op jit(solution)/shard_map/scatter-add | solution.py:95
  118.0 2.7 gather_fusion.33
  124.0 2.5 convolution_multiply_fusion.5
  127.8 1.9 convolution_multiply_fusion.3
  132.9 5.2 gather_fusion.34
  139.1 6.6 %scatter_custom_fusion.15 = f32[1536,64]{1,0:T(8,128)S(1)} fusion(s32[768]{0:T(1024)} %copy-done.80, f32[768,64]{1,0:T(8,128)} %bitcast.264, f32[]{:T(128)} %constant.22.clone.1), kind=kCustom, calls=%fused_computation.135 | custom fusion | flops 49152 | bytes 393728 | tf_op jit(solution)/shard_map/scatter-add | solution.py:95
  160.8 4.5 multiply_reduce_fusion.3
  165.3 34.2 %all-reduce = (f32[]{:T(128)}, f32[]{:T(128)}) all-reduce(f32[]{:T(128)} %get-tuple-element.7, f32[]{:T(128)} %get-tuple-element.6), channel_id=1, replica_groups=mesh['variant'=2,'elem'=4,'sub'=4] {'elem','sub'}, use_global_device_ids=true, to_apply=%region_17.0 | all-reduce | flops 2 | bytes 16 | tf_op jit(solution)/shard_map/psum | solution.py:130
  200.8 2.2 fusion.48
  213.1 14.8 %scatter_custom_fusion.29 = f32[1024]{0:T(1024)S(1)} fusion(s32[2048]{0:T(1024)} %bitcast.273, f32[2048]{0:T(1024)S(1)} %bitcast.277, f32[]{:T(128)} %constant.22.clone.1), kind=kCustom, calls=%fused_computation.256 | custom fusion | flops 2048 | bytes 4608 | tf_op jit(solution)/shard_map/scatter-add | solution.py:119
  228.0 9.0 %psum.59 = f32[1024]{0:T(1024)} all-reduce(f32[1024]{0:T(1024)S(1)} %scatter_custom_fusion.29), channel_id=1, replica_groups=mesh['variant'=2,'elem'=4,'sub'=4] {'sub'}, use_global_device_ids=true, to_apply=%region_35.39 | all-reduce | flops 1024 | bytes 8192 | tf_op jit(solution)/shard_map/psum | solution.py:122
  245.4 2.3 gather_fusion.35
  250.2 2.3 collective-permute-start.8
  253.4 9.4 %all-gather.1 = f32[4,1,256]{2,1,0:T(1,128)S(1)} all-gather(f32[1,1,256]{2,1,0:T(1,128)S(1)} %convolution_bitcast_fusion.4), channel_id=1, replica_groups=mesh['variant'=2,'elem'=4,'sub'=4] {'sub'}, dimensions={0}, use_global_device_ids=true | all-gather | bytes 5120 | tf_op jit(solution)/shard_map/all_gather | solution.py:124
  262.8 8.6 %gather_fusion.37 = f32[2048]{0:T(1024)S(1)} fusion(f32[1024]{0:T(1024)S(1)} %bitcast.251, s32[2048]{0:T(1024)S(1)} %broadcast_clamp_fusion), kind=kCustom, calls=%fused_computation.11.clone | custom fusion | bytes 24576 | tf_op jit(solution)/shard_map/jit(_take)/gather | solution.py:125
  272.4 5.2 gather_fusion.36
  278.5 6.8 %scatter_custom_fusion.22 = f32[1536,64]{1,0:T(8,128)S(1)} fusion(s32[768]{0:T(1024)} %copy-done.80, f32[768,64]{1,0:T(8,128)} %bitcast.265, f32[]{:T(128)} %constant.22.clone.1), kind=kCustom, calls=%fused_computation.133 | custom fusion | flops 49152 | bytes 393728 | tf_op jit(solution)/shard_map/scatter-add | solution.py:95
  300.3 2.8 multiply_reduce_fusion.2
  303.1 30.5 %psum.60 = f32[]{:T(128)} all-reduce(f32[]{:T(128)} %get-tuple-element.73), channel_id=1, replica_groups=mesh['variant'=2,'elem'=4,'sub'=4] {'elem','sub'}, use_global_device_ids=true, to_apply=%region_37.41 | all-reduce | flops 1 | bytes 8 | tf_op jit(solution)/shard_map/psum | solution.py:130
  339.9 3.4 convolution_multiply_fusion.2
  343.3 1.9 convolution_multiply_fusion.1
  345.2 1.9 convolution_multiply_fusion
  352.2 2.3 gather_fusion.38
  363.4 2.1 collective-permute-start.12
  365.5 2.3 convolution_add_fusion.2
  372.5 5.2 gather_fusion.39
  378.7 7.0 %scatter_custom_fusion.30 = f32[1536,64]{1,0:T(8,128)S(1)} fusion(s32[768]{0:T(1024)} %copy-done.80, f32[768,64]{1,0:T(8,128)} %bitcast.266, f32[]{:T(128)} %constant.22.clone.1), kind=kCustom, calls=%fused_computation.131 | custom fusion | flops 49152 | bytes 393728 | tf_op jit(solution)/shard_map/scatter-add | solution.py:95
  398.7 4.4 multiply_reduce_fusion.1
  403.1 32.5 %psum.61 = f32[]{:T(128)} all-reduce(f32[]{:T(128)} %get-tuple-element.75), channel_id=1, replica_groups=mesh['variant'=2,'elem'=4,'sub'=4] {'elem','sub'}, use_global_device_ids=true, to_apply=%region_46.50 | all-reduce | flops 1 | bytes 8 | tf_op jit(solution)/shard_map/psum | solution.py:130
  436.9 2.2 fusion.47
  449.1 14.8 %scatter_custom_fusion.44 = f32[1024]{0:T(1024)S(1)} fusion(s32[2048]{0:T(1024)} %bitcast.274, f32[2048]{0:T(1024)S(1)} %bitcast.275, f32[]{:T(128)} %constant.22.clone.1), kind=kCustom, calls=%fused_computation.254 | custom fusion | flops 2048 | bytes 4608 | tf_op jit(solution)/shard_map/scatter-add | solution.py:119
  464.0 8.4 %psum.62 = f32[1024]{0:T(1024)S(1)} all-reduce(f32[1024]{0:T(1024)S(1)} %scatter_custom_fusion.44), channel_id=1, replica_groups=mesh['variant'=2,'elem'=4,'sub'=4] {'sub'}, use_global_device_ids=true, to_apply=%region_55.59 | all-reduce | flops 1024 | bytes 8192 | tf_op jit(solution)/shard_map/psum | solution.py:122
  480.9 2.3 gather_fusion.40
  486.7 2.3 collective-permute-start.16
  489.9 9.6 %all-gather.2 = f32[4,1,256]{2,1,0:T(1,128)S(1)} all-gather(f32[1,1,256]{2,1,0:T(1,128)S(1)} %convolution_bitcast_fusion.3), channel_id=1, replica_groups=mesh['variant'=2,'elem'=4,'sub'=4] {'sub'}, dimensions={0}, use_global_device_ids=true | all-gather | bytes 5120 | tf_op jit(solution)/shard_map/all_gather | solution.py:124
  499.5 8.6 %gather_fusion.42 = f32[2048]{0:T(1024)S(1)} fusion(f32[1024]{0:T(1024)S(1)} %bitcast.249, s32[2048]{0:T(1024)S(1)} %broadcast_clamp_fusion), kind=kCustom, calls=%fused_computation.12.clone | custom fusion | bytes 24576 | tf_op jit(solution)/shard_map/jit(_take)/gather | solution.py:125
  508.5 5.2 gather_fusion.41
  514.6 6.6 %scatter_custom_fusion.37 = f32[1536,64]{1,0:T(8,128)S(1)} fusion(s32[768]{0:T(1024)} %copy-done.80, f32[768,64]{1,0:T(8,128)} %bitcast.262, f32[]{:T(128)} %constant.22.clone.1), kind=kCustom, calls=%fused_computation.129 | custom fusion | flops 49152 | bytes 393728 | tf_op jit(solution)/shard_map/scatter-add | solution.py:95
  534.2 2.9 multiply_reduce_fusion
  537.1 30.5 %psum.63 = f32[]{:T(128)} all-reduce(f32[]{:T(128)} %get-tuple-element.77), channel_id=1, replica_groups=mesh['variant'=2,'elem'=4,'sub'=4] {'elem','sub'}, use_global_device_ids=true, to_apply=%region_57.61 | all-reduce | flops 1 | bytes 8 | tf_op jit(solution)/shard_map/psum | solution.py:130
  (457 shorter events, 188.9 us)
Async XLA Ops:
  0.6 53.2 %copy-start = (f32[1,256,1024]{2,1,0:T(8,128)S(1)}, f32[1,256,1024]{2,1,0:T(8,128)}, u32[]{:S(2)}) copy-start(f32[1,256,1024]{2,1,0:T(8,128)} %param.153) | copy-start | bytes 3145732
  0.7 5.1 copy-start.61
  2.1 7.8 %copy-start.28 = (pred[4,192]{1,0:T(4,128)(4,1)}, pred[4,192]{1,0:T(4,128)(4,1)S(1)}, u32[]{:S(2)}) copy-start(pred[4,192]{1,0:T(4,128)(4,1)S(1)} %compare_and_fusion.1) | copy-start | bytes 2308
  9.9 10.2 %copy-start.38 = (s32[1,4,192]{2,1,0:T(4,128)S(1)}, s32[1,4,192]{2,1,0:T(4,128)}, u32[]{:S(2)}) copy-start(s32[1,4,192]{2,1,0:T(4,128)} %param.155) | copy-start | bytes 9220
  9.9 10.3 %copy-start.72 = (s32[1,4,192]{2,1,0:T(4,128)S(1)}, s32[1,4,192]{2,1,0:T(4,128)}, u32[]{:S(2)}) copy-start(s32[1,4,192]{2,1,0:T(4,128)} %param.156) | copy-start | bytes 9220
  9.9 10.8 %copy-start.27 = (s32[8,256]{1,0:T(8,128)S(1)}, s32[8,256]{1,0:T(8,128)}, u32[]{:S(2)}) copy-start(s32[8,256]{1,0:T(8,128)} %param.154) | copy-start | bytes 24580
  10.1 18.8 %copy-start.13 = (f32[256,512]{1,0:T(8,128)S(1)}, f32[256,512]{1,0:T(8,128)}, u32[]{:S(2)}) copy-start(f32[256,512]{1,0:T(8,128)} %param.149) | copy-start | bytes 1572868
  10.1 18.8 %copy-start.20 = (f32[512,8]{1,0:T(8,128)S(1)}, f32[512,8]{1,0:T(8,128)}, u32[]{:S(2)}) copy-start(f32[512,8]{1,0:T(8,128)} %constant.46.clone) | copy-start | bytes 49156
  10.8 69.7 %collective-permute-start.3 = (f32[96,128]{1,0:T(8,128)}, f32[96,128]{1,0:T(8,128)}, u32[]{:S(2)}, u32[]{:S(2)}) collective-permute-start(f32[96,128]{1,0:T(8,128)} %squeeze.100), channel_id=1, source_target_pairs={{0,8},{1,9},{2,10},{3,11},{4,12},{5,13},{6,14},{7,15},{8,0},{9,1},... | collective-permute-start | bytes 147464 | tf_op jit(solution)/shard_map/ppermute | solution.py:16
  14.5 66.9 %collective-permute-start.2 = (f32[96,128]{1,0:T(8,128)}, f32[96,128]{1,0:T(8,128)}, u32[]{:S(2)}, u32[]{:S(2)}) collective-permute-start(f32[96,128]{1,0:T(8,128)} %squeeze.99), channel_id=1, source_target_pairs={{0,4},{1,5},{2,6},{3,7},{4,0},{5,1},{6,2},{7,3},{8,12},{9,13},{10,... | collective-permute-start | bytes 147464 | tf_op jit(solution)/shard_map/ppermute | solution.py:16
  15.2 67.1 %collective-permute-start.1 = (f32[96,128]{1,0:T(8,128)}, f32[96,128]{1,0:T(8,128)}, u32[]{:S(2)}, u32[]{:S(2)}) collective-permute-start(f32[96,128]{1,0:T(8,128)} %squeeze.98), channel_id=1, source_target_pairs={{0,2},{1,3},{2,0},{3,1},{4,6},{5,7},{6,4},{7,5},{8,10},{9,11},{10,... | collective-permute-start | bytes 147464 | tf_op jit(solution)/shard_map/ppermute | solution.py:16
  18.5 64.7 %collective-permute-start = (f32[96,128]{1,0:T(8,128)}, f32[96,128]{1,0:T(8,128)}, u32[]{:S(2)}, u32[]{:S(2)}) collective-permute-start(f32[96,128]{1,0:T(8,128)} %squeeze.97), channel_id=1, source_target_pairs={{0,1},{1,0},{2,3},{3,2},{4,5},{5,4},{6,7},{7,6},{8,9},{9,8},{10,11... | collective-permute-start | bytes 147464 | tf_op jit(solution)/shard_map/ppermute | solution.py:16
  28.9 25.9 %copy-start.26 = (f32[64,256]{0,1:T(8,128)S(1)}, f32[64,256]{0,1:T(8,128)}, u32[]{:S(2)}) copy-start(f32[64,256]{0,1:T(8,128)} %get-tuple-element.43) | copy-start | bytes 196612
  28.9 26.0 %copy-start.25 = (f32[64,256]{0,1:T(8,128)S(1)}, f32[64,256]{0,1:T(8,128)}, u32[]{:S(2)}) copy-start(f32[64,256]{0,1:T(8,128)} %get-tuple-element.42) | copy-start | bytes 196612
  28.9 26.0 %copy-start.24 = (f32[64,256]{0,1:T(8,128)S(1)}, f32[64,256]{0,1:T(8,128)}, u32[]{:S(2)}) copy-start(f32[64,256]{0,1:T(8,128)} %get-tuple-element.41) | copy-start | bytes 196612
  29.0 25.8 %copy-start.79 = (s32[1,2,8,128]{3,1,2,0:T(2,128)}, s32[1,2,8,128]{3,1,2,0:T(2,128)S(1)}, u32[]{:S(2)}) copy-start(s32[1,2,8,128]{3,1,2,0:T(2,128)S(1)} %copy.358) | copy-start | bytes 24580
  29.5 26.9 %copy-start.68 = (s32[64]{0:T(128)S(1)}, s32[64]{0:T(128)}, u32[]{:S(2)}) copy-start(s32[64]{0:T(128)} %constant.152) | copy-start | bytes 772
  62.5 237.8 %copy-start.1 = (f32[256,512]{1,0:T(8,128)}, f32[256,512]{1,0:T(8,128)S(1)}, u32[]{:S(2)}) copy-start(f32[256,512]{1,0:T(8,128)S(1)} %copy.283) | copy-start | bytes 1572868
  84.1 5.3 copy-start.33
  122.0 10.6 %collective-permute-start.7 = (f32[96,128]{1,0:T(8,128)S(1)}, f32[96,128]{1,0:T(8,128)S(1)}, u32[]{:S(2)}, u32[]{:S(2)}) collective-permute-start(f32[96,128]{1,0:T(8,128)S(1)} %squeeze.111), channel_id=1, source_target_pairs={{0,8},{1,9},{2,10},{3,11},{4,12},{5,13},{6,14},{7,15},{8,0},{9,1},... | collective-permute-start | bytes 147464 | tf_op jit(solution)/shard_map/ppermute | solution.py:16
  122.6 10.0 %collective-permute-start.6 = (f32[96,128]{1,0:T(8,128)S(1)}, f32[96,128]{1,0:T(8,128)S(1)}, u32[]{:S(2)}, u32[]{:S(2)}) collective-permute-start(f32[96,128]{1,0:T(8,128)S(1)} %squeeze.110), channel_id=1, source_target_pairs={{0,4},{1,5},{2,6},{3,7},{4,0},{5,1},{6,2},{7,3},{8,12},{9,13},{10,... | collective-permute-start | bytes 147464 | tf_op jit(solution)/shard_map/ppermute | solution.py:16
  122.8 9.9 %collective-permute-start.5 = (f32[96,128]{1,0:T(8,128)S(1)}, f32[96,128]{1,0:T(8,128)S(1)}, u32[]{:S(2)}, u32[]{:S(2)}) collective-permute-start(f32[96,128]{1,0:T(8,128)S(1)} %squeeze.109), channel_id=1, source_target_pairs={{0,2},{1,3},{2,0},{3,1},{4,6},{5,7},{6,4},{7,5},{8,10},{9,11},{10,... | collective-permute-start | bytes 147464 | tf_op jit(solution)/shard_map/ppermute | solution.py:16
  123.0 9.8 %collective-permute-start.4 = (f32[96,128]{1,0:T(8,128)S(1)}, f32[96,128]{1,0:T(8,128)S(1)}, u32[]{:S(2)}, u32[]{:S(2)}) collective-permute-start(f32[96,128]{1,0:T(8,128)S(1)} %squeeze.108), channel_id=1, source_target_pairs={{0,1},{1,0},{2,3},{3,2},{4,5},{5,4},{6,7},{7,6},{8,9},{9,8},{10,11... | collective-permute-start | bytes 147464 | tf_op jit(solution)/shard_map/ppermute | solution.py:16
  132.9 5.3 copy-start.34
  150.2 4.7 copy-start.51
  160.8 40.0 %copy-start.14 = (f32[256,512]{1,0:T(8,128)S(1)}, f32[256,512]{1,0:T(8,128)}, u32[]{:S(2)}) copy-start(f32[256,512]{1,0:T(8,128)} %param.149) | copy-start | bytes 1572868
  247.6 4.9 copy-start.71
  248.9 23.1 %collective-permute-start.11 = (f32[96,128]{1,0:T(8,128)S(1)}, f32[96,128]{1,0:T(8,128)S(1)}, u32[]{:S(2)}, u32[]{:S(2)}) collective-permute-start(f32[96,128]{1,0:T(8,128)S(1)} %squeeze.115), channel_id=1, source_target_pairs={{0,8},{1,9},{2,10},{3,11},{4,12},{5,13},{6,14},{7,15},{8,0},{9,1},... | collective-permute-start | bytes 147464 | tf_op jit(solution)/shard_map/ppermute | solution.py:16
  249.6 22.5 %collective-permute-start.10 = (f32[96,128]{1,0:T(8,128)S(1)}, f32[96,128]{1,0:T(8,128)S(1)}, u32[]{:S(2)}, u32[]{:S(2)}) collective-permute-start(f32[96,128]{1,0:T(8,128)S(1)} %squeeze.114), channel_id=1, source_target_pairs={{0,4},{1,5},{2,6},{3,7},{4,0},{5,1},{6,2},{7,3},{8,12},{9,13},{10,... | collective-permute-start | bytes 147464 | tf_op jit(solution)/shard_map/ppermute | solution.py:16
  249.7 22.4 %collective-permute-start.9 = (f32[96,128]{1,0:T(8,128)S(1)}, f32[96,128]{1,0:T(8,128)S(1)}, u32[]{:S(2)}, u32[]{:S(2)}) collective-permute-start(f32[96,128]{1,0:T(8,128)S(1)} %squeeze.113), channel_id=1, source_target_pairs={{0,2},{1,3},{2,0},{3,1},{4,6},{5,7},{6,4},{7,5},{8,10},{9,11},{10,... | collective-permute-start | bytes 147464 | tf_op jit(solution)/shard_map/ppermute | solution.py:16
  250.2 22.1 %collective-permute-start.8 = (f32[96,128]{1,0:T(8,128)S(1)}, f32[96,128]{1,0:T(8,128)S(1)}, u32[]{:S(2)}, u32[]{:S(2)}) collective-permute-start(f32[96,128]{1,0:T(8,128)S(1)} %squeeze.112), channel_id=1, source_target_pairs={{0,1},{1,0},{2,3},{3,2},{4,5},{5,4},{6,7},{7,6},{8,9},{9,8},{10,11... | collective-permute-start | bytes 147464 | tf_op jit(solution)/shard_map/ppermute | solution.py:16
  272.4 5.3 copy-start.35
  354.4 11.1 %copy-start.9 = (f32[512,512]{1,0:T(8,128)S(1)}, f32[512,512]{1,0:T(8,128)}, u32[]{:S(2)}) copy-start(f32[512,512]{1,0:T(8,128)} %constant.82) | copy-start | bytes 3145732
  358.0 11.7 %collective-permute-start.15 = (f32[96,128]{1,0:T(8,128)}, f32[96,128]{1,0:T(8,128)}, u32[]{:S(2)}, u32[]{:S(2)}) collective-permute-start(f32[96,128]{1,0:T(8,128)} %squeeze.119), channel_id=1, source_target_pairs={{0,8},{1,9},{2,10},{3,11},{4,12},{5,13},{6,14},{7,15},{8,0},{9,1},... | collective-permute-start | bytes 147464 | tf_op jit(solution)/shard_map/ppermute | solution.py:16
  361.1 9.5 %collective-permute-start.14 = (f32[96,128]{1,0:T(8,128)}, f32[96,128]{1,0:T(8,128)}, u32[]{:S(2)}, u32[]{:S(2)}) collective-permute-start(f32[96,128]{1,0:T(8,128)} %squeeze.118), channel_id=1, source_target_pairs={{0,4},{1,5},{2,6},{3,7},{4,0},{5,1},{6,2},{7,3},{8,12},{9,13},{10,... | collective-permute-start | bytes 147464 | tf_op jit(solution)/shard_map/ppermute | solution.py:16
  362.7 8.8 %collective-permute-start.13 = (f32[96,128]{1,0:T(8,128)}, f32[96,128]{1,0:T(8,128)}, u32[]{:S(2)}, u32[]{:S(2)}) collective-permute-start(f32[96,128]{1,0:T(8,128)} %squeeze.117), channel_id=1, source_target_pairs={{0,2},{1,3},{2,0},{3,1},{4,6},{5,7},{6,4},{7,5},{8,10},{9,11},{10,... | collective-permute-start | bytes 147464 | tf_op jit(solution)/shard_map/ppermute | solution.py:16
  363.4 4.4 copy-start.12
  363.4 4.4 copy-start.22
  363.4 8.9 %collective-permute-start.12 = (f32[96,128]{1,0:T(8,128)}, f32[96,128]{1,0:T(8,128)S(1)}, u32[]{:S(2)}, u32[]{:S(2)}) collective-permute-start(f32[96,128]{1,0:T(8,128)} %squeeze.116), channel_id=1, source_target_pairs={{0,1},{1,0},{2,3},{3,2},{4,5},{5,4},{6,7},{7,6},{8,9},{9,8},{10,11... | collective-permute-start | bytes 147464 | tf_op jit(solution)/shard_map/ppermute | solution.py:16
  372.5 5.3 copy-start.36
  398.7 38.2 %copy-start.5 = (f32[256,512]{1,0:T(8,128)S(1)}, f32[256,512]{1,0:T(8,128)}, u32[]{:S(2)}) copy-start(f32[256,512]{1,0:T(8,128)} %param.150) | copy-start | bytes 1572868
  439.0 8.6 %copy-start.17 = (f32[256,512]{1,0:T(8,128)}, f32[256,512]{1,0:T(8,128)S(1)}, u32[]{:S(2)}) copy-start(f32[256,512]{1,0:T(8,128)S(1)} %get-tuple-element.11) | copy-start | bytes 1572868
  484.4 23.6 %collective-permute-start.19 = (f32[96,128]{1,0:T(8,128)S(1)}, f32[96,128]{1,0:T(8,128)S(1)}, u32[]{:S(2)}, u32[]{:S(2)}) collective-permute-start(f32[96,128]{1,0:T(8,128)S(1)} %squeeze.123), channel_id=1, source_target_pairs={{0,8},{1,9},{2,10},{3,11},{4,12},{5,13},{6,14},{7,15},{8,0},{9,1},... | collective-permute-start | bytes 147464 | tf_op jit(solution)/shard_map/ppermute | solution.py:16
  486.1 22.1 %collective-permute-start.18 = (f32[96,128]{1,0:T(8,128)S(1)}, f32[96,128]{1,0:T(8,128)S(1)}, u32[]{:S(2)}, u32[]{:S(2)}) collective-permute-start(f32[96,128]{1,0:T(8,128)S(1)} %squeeze.122), channel_id=1, source_target_pairs={{0,4},{1,5},{2,6},{3,7},{4,0},{5,1},{6,2},{7,3},{8,12},{9,13},{10,... | collective-permute-start | bytes 147464 | tf_op jit(solution)/shard_map/ppermute | solution.py:16
  486.2 22.0 %collective-permute-start.17 = (f32[96,128]{1,0:T(8,128)S(1)}, f32[96,128]{1,0:T(8,128)S(1)}, u32[]{:S(2)}, u32[]{:S(2)}) collective-permute-start(f32[96,128]{1,0:T(8,128)S(1)} %squeeze.121), channel_id=1, source_target_pairs={{0,2},{1,3},{2,0},{3,1},{4,6},{5,7},{6,4},{7,5},{8,10},{9,11},{10,... | collective-permute-start | bytes 147464 | tf_op jit(solution)/shard_map/ppermute | solution.py:16
  486.7 21.7 %collective-permute-start.16 = (f32[96,128]{1,0:T(8,128)S(1)}, f32[96,128]{1,0:T(8,128)S(1)}, u32[]{:S(2)}, u32[]{:S(2)}) collective-permute-start(f32[96,128]{1,0:T(8,128)S(1)} %squeeze.120), channel_id=1, source_target_pairs={{0,1},{1,0},{2,3},{3,2},{4,5},{5,4},{6,7},{7,6},{8,9},{9,8},{10,11... | collective-permute-start | bytes 147464 | tf_op jit(solution)/shard_map/ppermute | solution.py:16
  508.5 5.3 copy-start.37
  521.3 6.0 %copy-start.70 = (s32[64]{0:T(128)S(1)}, s32[64]{0:T(128)}, u32[]{:S(2)}) copy-start(s32[64]{0:T(128)} %constant.152) | copy-start | bytes 772
  (53 other events, 99.2 us)
where the time goes:
time: 581 us; the launch traced here: 570 us
  blocking collectives  182 us (31%)
  local copies, waits for them, and re-layouts  171 us (29%)
  other arithmetic  146 us (25%)
  matrix products  42.3 us (7%)
  starting transfers between devices  20.2 us (3%)
  between operations  8.42 us (1%)
    psum x4, blocking collectives, inner_total(): return lax.psum(jnp.sum(product), ('elem', 'sub'))  128 us
    scatter-add x3, other arithmetic, coarse_term(): jax.ops.segment_sum(corners.T.reshape(-1), vertex_ids.reshape(-1), num_se...  44.3 us
    scatter-add x36, other arithmetic, spread_faces(): result.at[:, sides[side_number]]  42.8 us
    scatter-add x6, other arithmetic, spread_faces(): flat = jnp.zeros((6 * count, square), values.dtype).at[slots.reshape(-1)]...  39.9 us
    all_gather x3, blocking collectives, coarse_term(): everywhere = lax.all_gather(solved, 'sub', axis=0, tiled=True)  28.3 us
    gather x30, local copies, waits for them, and re-layouts, face_values(): field[:, sides[side_number]]  27.6 us
    gather x6, local copies, waits for them, and re-layouts, coarse_term(): picked = jnp.take(everywhere, vertex_ids, axis=0)  26.3 us
    gather x6, local copies, waits for them, and re-layouts, neighbour_sum(): aligned = jnp.take_along_axis(received, partners[:, :, None], axis=1)  26.3 us
  transfers between devices with their start and end apart: 20, of which 0 were waited for; matrix products, arithmetic and copies ran while one was open for 15% of the time, Pallas kernels for 0%

commit v1 on v0

v1 whole, which is shorter than its diff:
```python
import functools

import jax
import jax.numpy as jnp
import ml_dtypes
import numpy as np
from jax import lax
from jax.experimental import pallas as pl
from jax.experimental.pallas import tpu as pltpu
from jax.sharding import PartitionSpec as P

NP = 8
PTS = NP**3
SQ = NP * NP
SMOOTH = 0.125
MESH = pl.DeviceIdType.MESH
F32 = jnp.float32
BF16 = jnp.bfloat16


def derivative_table(points):
    nodes = -np.cos(np.pi * np.arange(points) / (points - 1))
    end_weights = np.ones(points)
    end_weights[0] = 2.0
    end_weights[-1] = 2.0
    table = np.zeros((points, points))
    for i in range(points):
        for j in range(points):
            if i != j:
                table[i, j] = (
                    end_weights[i] / end_weights[j] * (-1.0) ** (i + j) / (nodes[i] - nodes[j])
                )
        table[i, i] = -np.sum(table[i])
    return nodes, table


def halves(x):
    x = np.asarray(x, np.float32)
    hi = x.astype(ml_dtypes.bfloat16)
    lo = (x - hi.astype(np.float32)).astype(ml_dtypes.bfloat16)
    return hi, lo


def tables(nh):
    nodes, deriv = derivative_table(NP)
    unit = np.eye(NP)
    k0 = np.kron(deriv, np.eye(SQ))
    k1 = np.kron(np.eye(4), np.kron(deriv, unit))
    k2 = np.kron(np.eye(4 * NP), deriv)
    hats = np.stack([(1.0 - nodes) / 2.0, (1.0 + nodes) / 2.0]).T
    raw = (
        hats[:, None, None, :, None, None]
        * hats[None, :, None, None, :, None]
        * hats[None, None, :, None, None, :]
    ).reshape(PTS, 8)
    corner = raw / raw.sum(axis=0, keepdims=True)
    grid = np.arange(PTS).reshape(NP, NP, NP)
    inner = [grid[:, 0], grid[:, -1], grid[:, :, 0], grid[:, :, -1]]
    sel = np.zeros((PTS, 4 * SQ), np.float32)
    spread = np.zeros((4 * 2 * SQ, PTS), np.float32)
    for s, side in enumerate(inner):
        for j, p in enumerate(side.ravel()):
            sel[p, s * SQ + j] = 1.0
            spread[s * 2 * SQ + j, p] = 1.0
            spread[s * 2 * SQ + SQ + j, p] = 1.0
    k0h, k0l = halves(k0)
    k1h, k1l = halves(k1)
    k2h, k2l = halves(k2)
    wh, wl = halves(np.repeat(corner, nh, axis=1))
    w = np.concatenate([wh, wl], axis=1)
    hh, hl = halves(np.repeat(raw.T, nh, axis=0))
    hh = np.concatenate([hh, hh], axis=0)
    hl = np.concatenate([hl, hl], axis=0)
    one = ml_dtypes.bfloat16
    return (
        np.stack([k0h, k0l]),
        np.stack([k1h, k1l]),
        np.stack([k2h, k2l]),
        sel.astype(one),
        spread.astype(one),
        w,
        np.stack([hh, hl]),
    )


NN = (((1,), (0,)), ((), ()))
NT = (((1,), (1,)), ((), ()))
TN = (((0,), (0,)), ((), ()))


def mm(a, b, dims=NN):
    return lax.dot_general(a, b, dims, preferred_element_type=F32)


def split(x):
    hi = x.astype(BF16)
    lo = (x - hi.astype(F32)).astype(BF16)
    return hi, lo


def iota(shape, dim):
    return lax.broadcasted_iota(jnp.int32, shape, dim)


def kernel(
    n_elem, n_sub, sections, width, nh,
    rhs_ref, scale_ref, helm_ref, geo_ref, inv_ref, vid_ref, slot_ref, partner_ref, slots_ref,
    k0_ref, k1_ref, k2_ref, sel_ref, spread_ref, w_ref, hat_ref,
    x_ref, r_ref, d_ref,
    gather, scatter, stacked, arrived, degree, corner_low, corner_high, inv_half,
    fsend, frecv, part, solved_slots, total_slots,
    fsend_sem, frecv_sem, psend_sem, precv_sem, ssend_sem, srecv_sem, tsend_sem, trecv_sem,
):
    count = rhs_ref.shape[0]
    half = width // 2
    devices = n_elem * n_sub
    ch = 8 * nh
    elem = lax.axis_index("elem")
    sub = lax.axis_index("sub")
    me = elem * n_sub + sub

    def other(j):
        p = lax.rem(me + j, devices)
        return {"elem": lax.div(p, n_sub), "sub": lax.rem(p, n_sub)}

    barrier = pltpu.get_barrier_semaphore()

    def greet(j, carry):
        pl.semaphore_signal(barrier, inc=1, device_id=other(j), device_id_type=MESH)
        return carry

    lax.fori_loop(1, devices, greet, 0)

    low = iota((1, 128), 1) < SQ

    for b in range(sections):
        hit = partner_ref[b : b + 1, :] == iota((width, width), 0)
        order = jnp.sum(
            jnp.where(hit, slots_ref[b : b + 1, :].astype(F32), 0.0), axis=1, keepdims=True
        ).astype(jnp.int32)
        gather[b * width : (b + 1) * width, :] = jnp.where(
            order == iota((width, 6 * count), 1), 1.0, 0.0
        ).astype(BF16)
    for s in range(6):
        scatter[s * count : (s + 1) * count, :] = jnp.where(
            slot_ref[...] - s * count == iota((count, sections * width), 0), 1.0, 0.0
        ).astype(BF16)

    vid = vid_ref[...]
    vid_high = lax.div(vid, 128)
    vid_low = vid - 128 * vid_high
    wide = iota((8, 8 * 128), 1)
    expand_low = jnp.where(lax.div(wide, 128) == iota((8, 8 * 128), 0), 1.0, 0.0)
    spread_low = mm(vid_low.astype(F32), expand_low, TN).astype(jnp.int32)
    corner_low[...] = jnp.where(
        spread_low == lax.rem(iota((count, 8 * 128), 1), 128), 1.0, 0.0
    ).astype(BF16)
    pair = iota((8, 2 * ch), 1)
    expand_high = jnp.where(lax.div(lax.rem(pair, ch), nh) == iota((8, 2 * ch), 0), 1.0, 0.0)
    spread_high = mm(vid_high.astype(F32), expand_high, TN).astype(jnp.int32)
    corner_high[...] = jnp.where(spread_high == lax.rem(iota((count, 2 * ch), 1), nh), 1.0, 0.0)

    inv_h, inv_l = split(inv_ref[...])
    inv_half[0] = inv_h
    inv_half[1] = inv_l

    def scatter_faces():
        flat = mm(scatter[...], arrived[...])
        sides = [flat[s * count : (s + 1) * count, :] for s in range(6)]
        inner = jnp.concatenate(sides[2:], axis=1).astype(BF16)
        result = mm(inner, spread_ref[...])
        first = sides[0] + pltpu.roll(sides[0], SQ, 1)
        last = sides[1] + pltpu.roll(sides[1], SQ, 1)
        return jnp.concatenate(
            [
                result[:, :128] + jnp.where(low, first, 0.0),
                result[:, 128 : PTS - 128],
                result[:, PTS - 128 :] + jnp.where(low, 0.0, last),
            ],
            axis=1,
        )

    arrived[...] = jnp.broadcast_to(jnp.where(low, 1.0, 0.0), arrived.shape).astype(BF16)
    degree[...] = scatter_faces()

    pl.semaphore_wait(barrier, devices - 1)

    pending = []

    def send_faces(step, v):
        hi = v.astype(BF16)
        hi_f = hi.astype(F32)
        lo_f = v - hi_f
        picked = mm(jnp.concatenate([hi, lo_f.astype(BF16)], axis=0), sel_ref[...])

        def lower(h, l):
            return jnp.where(low, h, pltpu.roll(l, SQ, 1)).astype(BF16)

        def upper(h, l):
            return jnp.where(low, pltpu.roll(h, SQ, 1), l).astype(BF16)

        stacked[0:count, :] = lower(hi_f[:, :128], lo_f[:, :128])
        stacked[count : 2 * count, :] = upper(hi_f[:, PTS - 128 :], lo_f[:, PTS - 128 :])
        for s in range(2):
            h = picked[:count, 128 * s : 128 * s + 128]
            l = picked[count:, 128 * s : 128 * s + 128]
            stacked[(2 + 2 * s) * count : (3 + 2 * s) * count, :] = lower(h, l)
            stacked[(3 + 2 * s) * count : (4 + 2 * s) * count, :] = upper(h, l)
        for b in reversed(range(sections)):
            rows = mm(gather[b * width : (b + 1) * width, :], stacked[...])
            rows = rows + pltpu.roll(rows, SQ, 1)
            fsend[step, b] = jnp.where(low, rows[:half], rows[half:])
            bit = lax.rem(lax.div(me, 2**b), 2)
            p = me + (1 - 2 * bit) * 2**b
            copy = pltpu.make_async_remote_copy(
                src_ref=fsend.at[step, b],
                dst_ref=frecv.at[step, b],
                send_sem=fsend_sem.at[step, b],
                recv_sem=frecv_sem.at[step, b],
                device_id={"elem": lax.div(p, n_sub), "sub": lax.rem(p, n_sub)},
                device_id_type=MESH,
            )
            copy.start()
            pending.append(copy)

    def neighbours(step):
        for b in reversed(range(sections)):
            pltpu.make_async_copy(
                frecv.at[step, b], frecv.at[step, b], frecv_sem.at[step, b]
            ).wait()
            v = frecv[step, b]
            hi = v.astype(BF16).astype(F32)
            lo = v - hi
            arrived[b * width : b * width + half, :] = jnp.where(
                low, hi, pltpu.roll(lo, SQ, 1)
            ).astype(BF16)
            arrived[b * width + half : (b + 1) * width, :] = jnp.where(
                low, pltpu.roll(hi, SQ, 1), lo
            ).astype(BF16)
        return scatter_faces()

    def to_sub_peers(step, slots, index_of, send_sem, recv_sem):
        for j in range(1, n_sub):
            copy = pltpu.make_async_remote_copy(
                src_ref=slots.at[step, index_of(0)],
                dst_ref=slots.at[step, index_of(j)],
                send_sem=send_sem.at[step, j],
                recv_sem=recv_sem.at[step, j],
                device_id={"elem": elem, "sub": lax.rem(sub + j, n_sub)},
                device_id_type=MESH,
            )
            copy.start()
            pending.append(copy)

    def wait_sub_peers(step, slots, recv_sem):
        for j in range(1, n_sub):
            pltpu.make_async_copy(slots.at[step, 0], slots.at[step, 0], recv_sem.at[step, j]).wait()

    def send_corners(step, r):
        hi, lo = split(r)
        y = mm(hi, w_ref[...]) + mm(lo, w_ref[...])
        y = (y + pltpu.roll(y, ch, 1)) * corner_high[...]
        hi = y.astype(BF16).astype(F32)
        both = jnp.where(iota((1, 2 * ch), 1) < ch, hi, y - hi).astype(BF16)
        products = mm(both, corner_low[...], TN)
        total = None
        for k in range(2):
            for c in range(8):
                piece = products[k * ch + c * nh : k * ch + (c + 1) * nh, 128 * c : 128 * c + 128]
                total = piece if total is None else total + piece
        part[step, 0] = total
        to_sub_peers(step, part, lambda j: j, psend_sem, precv_sem)

    def solve(step):
        wait_sub_peers(step, part, precv_sem)
        total = part[step, 0]
        for j in range(1, n_sub):
            total = total + part[step, j]
        hi = total.astype(BF16).astype(F32)
        lo = total - hi
        row_h = jnp.concatenate([hi[h : h + 1, :] for h in range(nh)], axis=1)
        row_l = jnp.concatenate([lo[h : h + 1, :] for h in range(nh)], axis=1)
        rows = jnp.concatenate([row_h, row_l, jnp.zeros((14, nh * 128), F32)], axis=0).astype(BF16)
        out = mm(rows, inv_half[0], NT) + mm(rows, inv_half[1], NT)
        out = out[0:1] + out[1:2]
        own = [out[:, 128 * k : 128 * k + 128] for k in range(out.shape[1] // 128)]
        own.append(jnp.zeros((8 - len(own), 128), F32))
        solved_slots[step, sub] = jnp.concatenate(own, axis=0)
        to_sub_peers(step, solved_slots, lambda j: sub, ssend_sem, srecv_sem)

    def coarse(step):
        wait_sub_peers(step, solved_slots, srecv_sem)
        each = nh // n_sub
        solved = jnp.concatenate([solved_slots[step, j, 0:each, :] for j in range(n_sub)], axis=0)
        hi = solved.astype(BF16).astype(F32)
        lo = solved - hi
        keep = lax.div(iota((ch, 8 * 128), 0), nh) == lax.div(iota((ch, 8 * 128), 1), 128)

        def blocks(x):
            column = jnp.concatenate([x] * 8, axis=0)
            return jnp.where(keep, jnp.concatenate([column] * 8, axis=1), 0.0).astype(BF16)

        spread = jnp.concatenate([blocks(hi), blocks(lo)], axis=0)
        picked = (mm(corner_low[...], spread, NT) * corner_high[...]).astype(BF16)
        return mm(picked, hat_ref[0]) + mm(picked, hat_ref[1])

    def local(v):
        n2 = PTS // 2
        hi, lo = split(v)
        k0h, k0l = k0_ref[0], k0_ref[1]

        def two(x):
            return jnp.concatenate([x[:, :n2], x[:, n2:]], axis=0)

        def three(h, l, kh, kl, dims):
            return mm(h, kh, dims) + mm(l, kh, dims) + mm(h, kl, dims)

        slope = geo_ref[0] * three(hi, lo, k0h, k0l, NT)
        sh, sl = split(slope)
        total = helm_ref[...] * v + three(sh, sl, k0h, k0l, NN)
        hi2, lo2 = two(hi), two(lo)
        rest = None
        for d, k in ((1, k1_ref), (2, k2_ref)):
            slope = two(geo_ref[d]) * three(hi2, lo2, k[0], k[1], NT)
            sh, sl = split(slope)
            piece = three(sh, sl, k[0], k[1], NN)
            rest = piece if rest is None else rest + piece
        return total + jnp.concatenate([rest[:count], rest[count:]], axis=1)

    def inner(a, b):
        return jnp.sum(a * b, axis=0, keepdims=True)

    def narrow(x):
        total = x[:, :128]
        for k in range(1, PTS // 128):
            total = total + x[:, 128 * k : 128 * k + 128]
        return total

    def send_totals(step, pairs):
        rows = [narrow(inner(a, b)) for a, b in pairs]
        rows.append(jnp.zeros((8 - len(rows), 128), F32))
        total_slots[step, 0] = jnp.concatenate(rows, axis=0)

        def start(j, carry):
            pltpu.make_async_remote_copy(
                src_ref=total_slots.at[step, 0],
                dst_ref=total_slots.at[step, j],
                send_sem=tsend_sem.at[step],
                recv_sem=trecv_sem.at[step],
                device_id=other(j),
                device_id_type=MESH,
            ).start()
            return carry

        lax.fori_loop(1, devices, start, 0)

    def totals(step, many):
        others = total_slots.at[step, pl.ds(1, devices - 1)]
        pltpu.make_async_copy(others, others, trecv_sem.at[step]).wait()
        whole = jnp.sum(total_slots[step], axis=0)
        sums = jnp.sum(whole, axis=1, keepdims=True)
        return [sums[k : k + 1] for k in range(many)]

    scale = scale_ref[...]

    def smooth_of(y, step):
        return scale * (y - SMOOTH * (degree[...] * y - neighbours(step)))

    def precondition(v, faces, step):
        y = scale * v
        send_corners(step, v)
        send_faces(faces, y)
        solve(step)
        smooth = smooth_of(y, faces)
        return smooth + coarse(step)

    def operator(v, step):
        send_faces(step, v)
        inside = local(v) + degree[...] * v
        return inside - neighbours(step)

    r0 = rhs_ref[...]
    z0 = precondition(r0, 0, 0)
    w0 = operator(z0, 1)
    send_totals(0, [(r0, z0), (z0, w0)])
    q0 = precondition(w0, 2, 1)
    rz0, dw0 = totals(0, 2)
    alpha0 = rz0 / dw0
    r1 = r0 - alpha0 * w0
    z1 = z0 - alpha0 * q0
    u1 = operator(z1, 3)
    send_totals(1, [(r1, z1), (z1, u1), (z1, w0), (z0, u1)])
    q1 = precondition(u1, 4, 2)
    rz1, zu, zw, du = totals(1, 4)
    beta0 = rz1 / rz0
    dw1 = zu + beta0 * (zw + du) + beta0 * beta0 * dw0
    alpha1 = rz1 / dw1
    d1 = z1 + beta0 * z0
    r2 = r1 - alpha1 * (u1 + beta0 * w0)
    z2 = z1 - alpha1 * (q1 + beta0 * q0)
    send_totals(2, [(r2, z2)])
    x_ref[...] = alpha0 * z0 + alpha1 * d1
    r_ref[...] = r2
    (rz2,) = totals(2, 1)
    d_ref[...] = z2 + (rz2 / rz1) * d1

    for copy in pending:
        copy.wait_send()
    for step in range(3):
        others = total_slots.at[step, pl.ds(1, devices - 1)]
        pltpu.make_async_copy(others, others, tsend_sem.at[step]).wait()


def on_device(
    n_elem, n_sub,
    right_side, smoother_scale, helmholtz, geometry, coarse_inverse, vertex_ids, face_slot, face_partner,
):
    count = right_side.shape[0]
    _, sections, width = face_slot.shape
    half = width // 2
    nv = coarse_inverse.shape[2]
    nh = nv // 128
    devices = n_elem * n_sub
    constants = [jnp.asarray(t) for t in tables(nh)]
    vmem = pl.BlockSpec(memory_space=pltpu.VMEM)
    field = jax.ShapeDtypeStruct((count, PTS), F32)
    dma = pltpu.SemaphoreType.DMA
    operands = (
        right_side, smoother_scale, helmholtz, geometry, coarse_inverse[0], vertex_ids,
        face_slot.reshape(1, sections * width), face_partner[0], face_slot[0], *constants,
    )
    return pl.pallas_call(
        functools.partial(kernel, n_elem, n_sub, sections, width, nh),
        out_shape=(field, field, field),
        in_specs=[vmem] * len(operands),
        out_specs=(vmem, vmem, vmem),
        scratch_shapes=[
            pltpu.VMEM((sections * width, 6 * count), BF16),
            pltpu.VMEM((6 * count, sections * width), BF16),
            pltpu.VMEM((6 * count, 128), BF16),
            pltpu.VMEM((sections * width, 128), BF16),
            pltpu.VMEM((count, PTS), F32),
            pltpu.VMEM((count, 8 * 128), BF16),
            pltpu.VMEM((count, 16 * nh), F32),
            pltpu.VMEM((2,) + coarse_inverse.shape[1:], BF16),
            pltpu.VMEM((5, sections, half, 128), F32),
            pltpu.VMEM((5, sections, half, 128), F32),
            pltpu.VMEM((3, n_sub, nh, 128), F32),
            pltpu.VMEM((3, n_sub, 8, 128), F32),
            pltpu.VMEM((3, devices, 8, 128), F32),
            dma((5, sections)),
            dma((5, sections)),
            dma((3, n_sub)),
            dma((3, n_sub)),
            dma((3, n_sub)),
            dma((3, n_sub)),
            dma((3,)),
            dma((3,)),
        ],
        compiler_params=pltpu.CompilerParams(
            collective_id=0, has_side_effects=True, vmem_limit_bytes=56 * 2**20
        ),
        cost_estimate=pl.CostEstimate(flops=2 * 10**10, bytes_accessed=8 * 10**6, transcendentals=0),
    )(*operands)


def solution(mesh):
    rows = P(("variant", "elem", "sub"), None)
    in_specs = (
        rows,
        rows,
        rows,
        P(None, ("variant", "elem", "sub"), None),
        P(("variant", "elem"), "sub", None),
        P(None, ("elem", "sub")),
        P(("elem", "sub"), None, None),
        P(("elem", "sub"), None, None),
    )
    body = functools.partial(on_device, mesh.shape["elem"], mesh.shape["sub"])
    return jax.shard_map(
        body, mesh=mesh, in_specs=in_specs, out_specs=(rows, rows, rows), check_vma=False
    )
```

time: 581 us -> 65.8 us (0.11); the launches traced: 570 us -> 65.6 us
  blocking collectives: 182 us -> 0 us
  local copies, waits for them, and re-layouts: 171 us -> 5.94 us
  other arithmetic: 146 us -> 0 us
  Pallas kernels: 0 us -> 59 us
  matrix products: 42.3 us -> 0 us
  starting transfers between devices: 20.2 us -> 0 us
  between operations: 8.42 us -> 0.65 us
    psum x7 -> x0, blocking collectives: 154 us -> none  [the longest x4 128 us: inner_total(): return lax.psum(jnp.sum(product), ('elem', 'sub'))]
    scatter-add x45 -> x0, other arithmetic: 127 us -> none  [the longest x3 44.3 us: coarse_term(): jax.ops.segment_sum(corners.T.reshape(-1), vertex_ids.reshape(-1), num_se...]
    gather x47 -> x0, local copies, waits for them, and re-layouts: 91.3 us -> none  [the longest x30 27.6 us: face_values(): field[:, sides[side_number]]]
    pallas_call x0 -> x1, Pallas kernels: none -> 59 us  [on_device(): pl.pallas_call(functools.partial(kernel, n_elem, n_sub, sections, width,...]
    dot_general x21 -> x0, matrix products: 42.3 us -> none  [the longest x6 15.9 us: stiffness(): jnp.dot(geometry[direction_index] * slope, operators[direction_index], pr...]
    all_gather x3 -> x0, blocking collectives: 28.3 us -> none  [coarse_term(): everywhere = lax.all_gather(solved, 'sub', axis=0, tiled=True)]
    slice x47 -> x0, local copies, waits for them, and re-layouts: 25.8 us -> none  [the longest x42 25 us: spread_faces(): flat[side_number * count:(side_number + 1) * count]]
    ppermute x20 -> x0, starting transfers between devices: 20.2 us -> none  [from_partner(): lax.ppermute(x, axis, [(i, i ^ 1 << distance) for i in range(lax.axis_siz...]
  transfers between devices with their start and end apart: 20 -> 0, of which waited for: 0 -> 0; matrix products, arithmetic and copies ran while one was open for 15% -> 0% of each run, Pallas kernels for 0% -> 0%
where the time goes in v1:
time: 65.8 us; the launch traced here: 65.6 us
  Pallas kernels  59 us (90%)
  local copies, waits for them, and re-layouts  5.94 us (9%)
    pallas_call x1, Pallas kernels, on_device(): pl.pallas_call(functools.partial(kernel, n_elem, n_sub, sections, width,...  59 us
    unnamed x5, local copies, waits for them, and re-layouts  4.59 us
    reshape x1, local copies, waits for them, and re-layouts, on_device(): face_slot.reshape(1, sections * width)  1.35 us

profile of v1, /device:TPU:0, one launch (start us, length us, event | category | flops | bytes accessed | tf_op | source)
XLA Modules:
  0.0 65.6 jit_solution(6795864708749580042)
XLA Ops:
  0.6 1.3 %reshape.9.slot_ref = s32[1,768]{1,0:T(1,128)} reshape(s32[1,4,192]{2,1,0:T(4,128)} %param.21) | data formatting | bytes 6144 | tf_op jit(solution)/shard_map/reshape | solution.py:430
  2.0 59.0 %shard_map.166 = (f32[256,512]{1,0:T(8,128)}, f32[256,512]{1,0:T(8,128)}, f32[256,512]{1,0:T(8,128)}) custom-call(f32[256,512]{1,0:T(8,128)} %rhs_ref.1, f32[256,512]{1,0:T(8,128)} %scale_ref.1, f32[256,512]{1,0:T(8,128)} %helm_ref.1, f32[3,256,512]{2,1,0:T(8,128)} %geo_ref.1, f32[256,1024]{1,0:T(8,128)} %bitcast.4, s32[8,256]{1,0:T(8,128)} %vid_ref.1, ...), custom_call_target="tpu_custom_call" | custom-call | flops 20000000000 | bytes 8000000 | tf_op jit(solution)/shard_map/pallas_call | solution.py:432
  61.0 0.0 copy-start
  61.0 1.9 %copy.21 = f32[256,512]{1,0:T(8,128)} copy(f32[256,512]{1,0:T(8,128)} %get-tuple-element.6) | data formatting | bytes 1048576
  62.9 1.9 %copy.22 = f32[256,512]{1,0:T(8,128)} copy(f32[256,512]{1,0:T(8,128)} %get-tuple-element.7) | data formatting | bytes 1048576
  64.8 0.0 copy-done
  64.8 0.8 %copy.23 = f32[256,512]{1,0:T(8,128)} copy(f32[256,512]{1,0:T(8,128)S(1)} %copy-done) | data formatting | bytes 1048576
Async XLA Ops:
  61.0 3.8 %copy-start = (f32[256,512]{1,0:T(8,128)S(1)}, f32[256,512]{1,0:T(8,128)}, u32[]{:S(2)}) copy-start(f32[256,512]{1,0:T(8,128)} %get-tuple-element.8) | copy-start | bytes 1572868

commit v2 on v1

--- a/solution.py
+++ b/solution.py
@@ -104,13 +104,25 @@
 
 def kernel(
     n_elem, n_sub, sections, width, nh,
-    rhs_ref, scale_ref, helm_ref, geo_ref, inv_ref, vid_ref, slot_ref, partner_ref, slots_ref,
-    k0_ref, k1_ref, k2_ref, sel_ref, spread_ref, w_ref, hat_ref,
+    rhs_ref, scale_ref, helm_hbm, geo_hbm, inv_hbm, vid_ref, partner_ref, slots_ref,
+    k0_hbm, k1_hbm, k2_hbm, sel_ref, spread_ref, w_ref, hat_ref,
     x_ref, r_ref, d_ref,
     gather, scatter, stacked, arrived, degree, corner_low, corner_high, inv_half,
     fsend, frecv, part, solved_slots, total_slots,
     fsend_sem, frecv_sem, psend_sem, precv_sem, ssend_sem, srecv_sem, tsend_sem, trecv_sem,
+    inv_ref, helm_ref, geo_ref, k0_ref, k1_ref, k2_ref, load_sem,
 ):
+    loads = [
+        pltpu.make_async_copy(src, dst, load_sem.at[k])
+        for k, (src, dst) in enumerate(
+            (
+                (inv_hbm, inv_ref), (k0_hbm, k0_ref), (geo_hbm, geo_ref),
+                (helm_hbm, helm_ref), (k1_hbm, k1_ref), (k2_hbm, k2_ref),
+            )
+        )
+    ]
+    for load in loads:
+        load.start()
     count = rhs_ref.shape[0]
     half = width // 2
     devices = n_elem * n_sub
@@ -141,9 +153,10 @@
         gather[b * width : (b + 1) * width, :] = jnp.where(
             order == iota((width, 6 * count), 1), 1.0, 0.0
         ).astype(BF16)
+    slot_row = jnp.concatenate([slots_ref[b : b + 1, :] for b in range(sections)], axis=1)
     for s in range(6):
         scatter[s * count : (s + 1) * count, :] = jnp.where(
-            slot_ref[...] - s * count == iota((count, sections * width), 0), 1.0, 0.0
+            slot_row - s * count == iota((count, sections * width), 0), 1.0, 0.0
         ).astype(BF16)
 
     vid = vid_ref[...]
@@ -159,10 +172,6 @@
     expand_high = jnp.where(lax.div(lax.rem(pair, ch), nh) == iota((8, 2 * ch), 0), 1.0, 0.0)
     spread_high = mm(vid_high.astype(F32), expand_high, TN).astype(jnp.int32)
     corner_high[...] = jnp.where(spread_high == lax.rem(iota((count, 2 * ch), 1), nh), 1.0, 0.0)
-
-    inv_h, inv_l = split(inv_ref[...])
-    inv_half[0] = inv_h
-    inv_half[1] = inv_l
 
     def scatter_faces():
         flat = mm(scatter[...], arrived[...])
@@ -183,9 +192,17 @@
     arrived[...] = jnp.broadcast_to(jnp.where(low, 1.0, 0.0), arrived.shape).astype(BF16)
     degree[...] = scatter_faces()
 
+    for load in loads:
+        load.wait()
+    inv_h, inv_l = split(inv_ref[...])
+    inv_half[0] = inv_h
+    inv_half[1] = inv_l
+
     pl.semaphore_wait(barrier, devices - 1)
 
     pending = []
+    inner_bits = n_sub.bit_length() - 1
+    send_order = list(reversed(range(inner_bits))) + list(range(inner_bits, sections))
 
     def send_faces(step, v):
         hi = v.astype(BF16)
@@ -206,7 +223,7 @@
             l = picked[count:, 128 * s : 128 * s + 128]
             stacked[(2 + 2 * s) * count : (3 + 2 * s) * count, :] = lower(h, l)
             stacked[(3 + 2 * s) * count : (4 + 2 * s) * count, :] = upper(h, l)
-        for b in reversed(range(sections)):
+        for b in send_order:
             rows = mm(gather[b * width : (b + 1) * width, :], stacked[...])
             rows = rows + pltpu.roll(rows, SQ, 1)
             fsend[step, b] = jnp.where(low, rows[:half], rows[half:])
@@ -224,7 +241,7 @@
             pending.append(copy)
 
     def neighbours(step):
-        for b in reversed(range(sections)):
+        for b in reversed(send_order):
             pltpu.make_async_copy(
                 frecv.at[step, b], frecv.at[step, b], frecv_sem.at[step, b]
             ).wait()
@@ -411,6 +428,19 @@
         pltpu.make_async_copy(others, others, tsend_sem.at[step]).wait()
 
 
+def hand_over(x_ref, r_ref, d_ref, x_out, r_out, d_out, sem):
+    rows = x_ref.shape[0] // 4
+    copies = []
+    for k, (src, dst) in enumerate(((x_ref, x_out), (r_ref, r_out), (d_ref, d_out))):
+        for q in range(4):
+            block = pl.ds(q * rows, rows)
+            copies.append(pltpu.make_async_copy(src.at[block], dst.at[block], sem.at[k, q]))
+    for copy in copies:
+        copy.start()
+    for copy in copies:
+        copy.wait()
+
+
 def on_device(
     n_elem, n_sub,
     right_side, smoother_scale, helmholtz, geometry, coarse_inverse, vertex_ids, face_slot, face_partner,
@@ -423,16 +453,17 @@
     devices = n_elem * n_sub
     constants = [jnp.asarray(t) for t in tables(nh)]
     vmem = pl.BlockSpec(memory_space=pltpu.VMEM)
+    hbm = pl.BlockSpec(memory_space=pl.ANY)
     field = jax.ShapeDtypeStruct((count, PTS), F32)
     dma = pltpu.SemaphoreType.DMA
     operands = (
         right_side, smoother_scale, helmholtz, geometry, coarse_inverse[0], vertex_ids,
-        face_slot.reshape(1, sections * width), face_partner[0], face_slot[0], *constants,
+        face_partner[0], face_slot[0], *constants,
     )
-    return pl.pallas_call(
+    results = pl.pallas_call(
         functools.partial(kernel, n_elem, n_sub, sections, width, nh),
         out_shape=(field, field, field),
-        in_specs=[vmem] * len(operands),
+        in_specs=[hbm if k in (2, 3, 4, 8, 9, 10) else vmem for k in range(len(operands))],
         out_specs=(vmem, vmem, vmem),
         scratch_shapes=[
             pltpu.VMEM((sections * width, 6 * count), BF16),
@@ -456,12 +487,28 @@
             dma((3, n_sub)),
             dma((3,)),
             dma((3,)),
+            pltpu.VMEM(coarse_inverse.shape[1:], F32),
+            pltpu.VMEM((count, PTS), F32),
+            pltpu.VMEM((3, count, PTS), F32),
+            pltpu.VMEM((2, PTS, PTS), BF16),
+            pltpu.VMEM((2, PTS // 2, PTS // 2), BF16),
+            pltpu.VMEM((2, PTS // 2, PTS // 2), BF16),
+            dma((6,)),
         ],
         compiler_params=pltpu.CompilerParams(
             collective_id=0, has_side_effects=True, vmem_limit_bytes=56 * 2**20
         ),
         cost_estimate=pl.CostEstimate(flops=2 * 10**10, bytes_accessed=8 * 10**6, transcendentals=0),
     )(*operands)
+    return pl.pallas_call(
+        hand_over,
+        out_shape=(field, field, field),
+        in_specs=[hbm] * 3,
+        out_specs=(hbm, hbm, hbm),
+        scratch_shapes=[dma((3, 4))],
+        compiler_params=pltpu.CompilerParams(vmem_limit_bytes=56 * 2**20),
+        cost_estimate=pl.CostEstimate(flops=0, bytes_accessed=3 * 2**20, transcendentals=0),
+    )(*results)
 
 
 def solution(mesh):

time: 65.8 us -> 108 us (1.64)
  Pallas kernels: 59 us -> 107 us
  local copies, waits for them, and re-layouts: 5.94 us -> 0 us
    pallas_call x0 -> x1, Pallas kernels: none -> 48.9 us  [on_device(): pl.pallas_call(hand_over, out_shape=(field, field, field), in_specs=[hbm]...]
    unnamed x5 -> x0, local copies, waits for them, and re-layouts: 4.59 us -> none
    reshape x1 -> x0, local copies, waits for them, and re-layouts: 1.35 us -> none  [on_device(): face_slot.reshape(1, sections * width)]
where the time goes in v2:
time: 108 us
  Pallas kernels  107 us (99%)
    pallas_call x1, Pallas kernels, on_device(): pl.pallas_call(functools.partial(kernel, n_elem, n_sub, sections, width,...  58.3 us
    pallas_call x1, Pallas kernels, on_device(): pl.pallas_call(hand_over, out_shape=(field, field, field), in_specs=[hbm]...  48.9 us

profile of v2, /device:TPU:0, one launch (start us, length us, event | category | flops | bytes accessed | tf_op | source)
XLA Modules:
  0.0 108.0 jit_solution(3876315373118611555)
XLA Ops:
  0.6 58.3 %shard_map.166 = (f32[256,512]{1,0:T(8,128)}, f32[256,512]{1,0:T(8,128)}, f32[256,512]{1,0:T(8,128)}) custom-call(f32[256,512]{1,0:T(8,128)} %rhs_ref.1, f32[256,512]{1,0:T(8,128)} %scale_ref.1, f32[256,512]{1,0:T(8,128)} %helm_hbm.1, f32[3,256,512]{2,1,0:T(8,128)} %geo_hbm.1, f32[256,1024]{1,0:T(8,128)} %bitcast.3, s32[8,256]{1,0:T(8,128)} %vid_ref.1, ...), custom_call_target="tpu_custom_call" | custom-call | flops 20000000000 | bytes 8000000 | tf_op jit(solution)/shard_map/pallas_call | solution.py:463
  58.9 48.9 %shard_map.167 = (f32[256,512]{1,0:T(8,128)}, f32[256,512]{1,0:T(8,128)}, f32[256,512]{1,0:T(8,128)}) custom-call(f32[256,512]{1,0:T(8,128)} %get-tuple-element.6.x_ref, f32[256,512]{1,0:T(8,128)} %get-tuple-element.7.r_ref, f32[256,512]{1,0:T(8,128)} %get-tuple-element.8.d_ref), custom_call_target="tpu_custom_call" | custom-call | bytes 3145728 | tf_op jit(solution)/shard_map/pallas_call | solution.py:503

commit v3 on v2

--- a/solution.py
+++ b/solution.py
@@ -428,17 +428,10 @@
         pltpu.make_async_copy(others, others, tsend_sem.at[step]).wait()
 
 
-def hand_over(x_ref, r_ref, d_ref, x_out, r_out, d_out, sem):
-    rows = x_ref.shape[0] // 4
-    copies = []
-    for k, (src, dst) in enumerate(((x_ref, x_out), (r_ref, r_out), (d_ref, d_out))):
-        for q in range(4):
-            block = pl.ds(q * rows, rows)
-            copies.append(pltpu.make_async_copy(src.at[block], dst.at[block], sem.at[k, q]))
-    for copy in copies:
-        copy.start()
-    for copy in copies:
-        copy.wait()
+def hand_over(x_ref, r_ref, d_ref, x_out, r_out, d_out):
+    x_out[...] = x_ref[...]
+    r_out[...] = r_ref[...]
+    d_out[...] = d_ref[...]
 
 
 def on_device(
@@ -454,6 +447,7 @@
     constants = [jnp.asarray(t) for t in tables(nh)]
     vmem = pl.BlockSpec(memory_space=pltpu.VMEM)
     hbm = pl.BlockSpec(memory_space=pl.ANY)
+    block = pl.BlockSpec((count // 2, PTS), lambda i: (i, 0))
     field = jax.ShapeDtypeStruct((count, PTS), F32)
     dma = pltpu.SemaphoreType.DMA
     operands = (
@@ -503,9 +497,9 @@
     return pl.pallas_call(
         hand_over,
         out_shape=(field, field, field),
-        in_specs=[hbm] * 3,
-        out_specs=(hbm, hbm, hbm),
-        scratch_shapes=[dma((3, 4))],
+        grid=(2,),
+        in_specs=[block] * 3,
+        out_specs=(block, block, block),
         compiler_params=pltpu.CompilerParams(vmem_limit_bytes=56 * 2**20),
         cost_estimate=pl.CostEstimate(flops=0, bytes_accessed=3 * 2**20, transcendentals=0),
     )(*results)

time: 108 us -> 61.4 us (0.57)
  Pallas kernels: 107 us -> 60.6 us
    pallas_call x1, Pallas kernels: 48.9 us -> 2.31 us  [on_device(): pl.pallas_call(hand_over, out_shape=(field, field, field), grid=(2,), in_...]
where the time goes in v3:
time: 61.4 us; the launch traced here: 61.2 us
  Pallas kernels  60.6 us (99%)
  between operations  0.64 us (1%)
    pallas_call x1, Pallas kernels, on_device(): pl.pallas_call(functools.partial(kernel, n_elem, n_sub, sections, width,...  58.3 us
    pallas_call x1, Pallas kernels, on_device(): pl.pallas_call(hand_over, out_shape=(field, field, field), grid=(2,), in_...  2.31 us

profile of v3, /device:TPU:0, one launch (start us, length us, event | category | flops | bytes accessed | tf_op | source)
XLA Modules:
  0.0 61.2 jit_solution(4740663423644882701)
XLA Ops:
  0.6 58.3 %shard_map.166 = (f32[256,512]{1,0:T(8,128)}, f32[256,512]{1,0:T(8,128)}, f32[256,512]{1,0:T(8,128)}) custom-call(f32[256,512]{1,0:T(8,128)} %rhs_ref.1, f32[256,512]{1,0:T(8,128)} %scale_ref.1, f32[256,512]{1,0:T(8,128)} %helm_hbm.1, f32[3,256,512]{2,1,0:T(8,128)} %geo_hbm.1, f32[256,1024]{1,0:T(8,128)} %bitcast.3, s32[8,256]{1,0:T(8,128)} %vid_ref.1, ...), custom_call_target="tpu_custom_call" | custom-call | flops 20000000000 | bytes 8000000 | tf_op jit(solution)/shard_map/pallas_call | solution.py:457
  58.9 2.3 %shard_map.167 = (f32[256,512]{1,0:T(8,128)}, f32[256,512]{1,0:T(8,128)}, f32[256,512]{1,0:T(8,128)}) custom-call(f32[256,512]{1,0:T(8,128)} %get-tuple-element.6.x_ref, f32[256,512]{1,0:T(8,128)} %get-tuple-element.7.r_ref, f32[256,512]{1,0:T(8,128)} %get-tuple-element.8.d_ref), custom_call_target="tpu_custom_call" | custom-call | bytes 3145728 | tf_op jit(solution)/shard_map/pallas_call | solution.py:497
